TPU v7x, 32 devices: a whole 2x2x4 slice. The times are simulated.
32 devices in a mesh: side: 2 (over y), grp: 8 (over z, x), tp: 2 (over core).
Axes of the slice: x: 2, y: 2, z: 4, core: 2. Of those that a mesh axis runs over, the one named last changes fastest.
Arguments:
- residual: bfloat16 [2, 128, 7168], P('side', 'grp'), may hold values from -14 to 14
- moe_gain: bfloat16 [2, 7168], P('side'), may hold values from 0.5 to 1.5
- router: bfloat16 [2, 16, 7168], P('side'), may hold values from -0.0625 to 0.0625
- routes: int32 [2, 128, 8], P('side', 'grp'), may hold values from 0 to 15, all different within a row; in each aligned block of 8 rows (0 to 7, 8 to 15, ..., all dimensions but the last counted through in order) at most 5 rows name the same one
- gate_w: bfloat16 [2, 7168, 16384], P('side', None, ('grp', 'tp')), may hold values from -0.0625 to 0.0625
- up_w: bfloat16 [2, 7168, 16384], P('side', None, ('grp', 'tp')), may hold values from -0.0625 to 0.0625
- down_w: bfloat16 [2, 16384, 7168], P('side', ('grp', 'tp')), may hold values from -0.1875 to 0.1875
- attn_gain: bfloat16 [2, 7168], P('side', 'tp'), may hold values from 0.5 to 1.5
- kv_proj: bfloat16 [2, 576, 7168], P('side', None, 'tp'), may hold values from -0.0625 to 0.0625
- kv_gain: bfloat16 [2, 512], P('side'), may hold values from 0.5 to 1.5
- cache_latent: bfloat16 [2, 128, 128, 512], P('side', 'grp'), may hold values from -5 to 5
- cache_rope: bfloat16 [2, 128, 64, 128], P('side', 'grp'), may hold values from -5 to 5
- lengths: int32 [2, 128], P('side', 'grp'), may hold values from 2 to 128, as said below
- query_latent: bfloat16 [2, 128, 64, 512], P('side', 'grp', 'tp'), may hold values from -34 to 34
- query_rope: bfloat16 [2, 128, 4096], P('side', 'grp', 'tp'), may hold values from -5 to 5
Outputs:
- resid_out: bfloat16 [2, 128, 7168], P('side', 'grp')
- new_latent: bfloat16 [2, 128, 512], P('side', 'grp')
- new_rope: bfloat16 [2, 128, 64], P('side', 'grp')
- attn_latent: bfloat16 [2, 128, 64, 512], P('side', 'grp', 'tp')
Inputs may be any that keep to these rules, and one draw needn't show every extreme that they name: `routes`: within each aligned block of 8 rows every row names 8 different experts and no expert is named by more than 5 rows of the block. `lengths`: every attention group's 16 sequences include one with exactly 128 cached tokens.
All inputs are finite; a program needn't handle non-finite values.
Results may differ from a plain program's by a relative error of at most 0.015.
Values may be sent and summed in bfloat16 or wider, within the bound.
A program may use at most 128 MiB of HBM per device.

v0:
```python
import jax
import jax.numpy as jnp
from jax import lax
from jax.sharding import PartitionSpec as P

NMB = 2
CAP = 5


NORM_EPS = 1e-06
ROUTE_SCALE = 2.5
ROPE_BASE = 10000.0
SCORE_SCALE = 192.0 ** (-0.5)


def rms_scale(values):
    return lax.rsqrt(jnp.mean(values * values, axis=-1, keepdims=True) + NORM_EPS)


def rotate(pair_part, position):
    half_width = pair_part.shape[-1] // 2
    step_ids = lax.broadcasted_iota(jnp.int32, (1, half_width), 1).astype(jnp.float32)
    inverse_freq = jnp.exp(-(2.0 * step_ids / pair_part.shape[-1]) * jnp.log(ROPE_BASE))
    angles = position.astype(jnp.float32)[:, None] * inverse_freq
    first_half = pair_part[:, :half_width]
    second_half = pair_part[:, half_width:]
    cosine = jnp.cos(angles)
    sine_part = jnp.sin(angles)
    return jnp.concatenate(
        [
            first_half * cosine - second_half * sine_part,
            first_half * sine_part + second_half * cosine,
        ],
        axis=-1,
    )


def mixing_tables(chosen, weight, targets, experts, capacity):
    expert_iota = lax.broadcasted_iota(jnp.int32, (1, 1, experts), 2)
    matches = (chosen[:, :, None] == expert_iota).astype(jnp.int32)
    per_row = jnp.sum(matches, axis=1)
    before = jnp.cumsum(per_row, axis=0) - per_row
    slots = jnp.sum(matches * before[:, None, :], axis=2)
    places = chosen * capacity + slots
    matching = places[None, None, :, :] == targets[:, :, None, None]
    row_count = chosen.shape[0]
    selector = jnp.any(matching, axis=3).astype(jnp.bfloat16).reshape(-1, row_count)
    mixing = jnp.einsum(
        "jcik,ik->ijc", matching.astype(jnp.bfloat16), weight, preferred_element_type=jnp.float32
    )
    return (selector, mixing.astype(jnp.bfloat16).reshape(row_count, -1))


def attend(operands):
    query_lat, query_rot, cache_lat, cache_rot, seq_lengths, fresh_lat, fresh_rot = operands
    head_count = query_lat.shape[1]
    query_rot = query_rot.reshape(query_rot.shape[0], head_count, -1)
    cache_scores = (
        jnp.einsum("thl,tpl->thp", query_lat, cache_lat, preferred_element_type=jnp.float32)
        + jnp.einsum("thr,trp->thp", query_rot, cache_rot, preferred_element_type=jnp.float32)
    ) * SCORE_SCALE
    own_scores = (
        jnp.einsum("thl,tl->th", query_lat, fresh_lat, preferred_element_type=jnp.float32)
        + jnp.einsum("thr,tr->th", query_rot, fresh_rot, preferred_element_type=jnp.float32)
    ) * SCORE_SCALE
    position_ids = lax.broadcasted_iota(jnp.int32, cache_scores.shape, 2)
    usable = position_ids < seq_lengths[:, None, None]
    cache_scores = jnp.where(usable, cache_scores, -1e30)
    peak = jnp.maximum(jnp.max(cache_scores, axis=2), own_scores)
    cache_weights = jnp.where(usable, jnp.exp(cache_scores - peak[:, :, None]), 0.0)
    own_weight = jnp.exp(own_scores - peak)
    denominator = jnp.sum(cache_weights, axis=2) + own_weight
    cache_probs = (cache_weights / denominator[:, :, None]).astype(jnp.bfloat16)
    own_probs = (own_weight / denominator).astype(jnp.bfloat16)
    mixed = jnp.einsum("thp,tpl->thl", cache_probs, cache_lat, preferred_element_type=jnp.float32)
    mixed = (
        mixed
        + own_probs.astype(jnp.float32)[:, :, None] * fresh_lat.astype(jnp.float32)[:, None, :]
    )
    return mixed.astype(jnp.bfloat16)


def body(
    residual,
    moe_gain,
    router,
    routes,
    gate_w,
    up_w,
    down_w,
    attn_gain,
    kv_proj,
    kv_gain,
    cache_latent,
    cache_rope,
    lengths,
    query_latent,
    query_rope,
):
    is_attn = lax.axis_index("side") == 0
    tp_index = lax.axis_index("tp")
    n_grp = lax.axis_size("grp")
    n_tp = lax.axis_size("tp")
    model_width = residual.shape[2]
    group_rows = residual.shape[1]
    rows_mb = group_rows // NMB
    experts = router.shape[1]
    expert_span = n_grp * n_tp // experts
    half_width = attn_gain.shape[1]
    latent_width = kv_gain.shape[1]
    heads_here = query_latent.shape[2]
    x_rows = residual[0].astype(jnp.float32)
    normed = x_rows * rms_scale(x_rows) * moe_gain[0].astype(jnp.float32)
    logits = jnp.dot(normed, router[0].astype(jnp.float32).T, precision=lax.Precision.HIGHEST)
    moe_in = normed.astype(jnp.bfloat16)
    scores = jax.nn.sigmoid(logits)
    chosen = routes[0]
    expert_iota = lax.broadcasted_iota(jnp.int32, (1, 1, experts), 2)
    picked = jnp.sum(jnp.where(chosen[:, :, None] == expert_iota, scores[:, None, :], 0.0), axis=2)
    weight = (ROUTE_SCALE * picked / jnp.sum(picked, axis=1, keepdims=True)).astype(jnp.bfloat16)
    dest_ids = lax.broadcasted_iota(jnp.int32, (n_grp, 1), 0)
    dest_expert = (dest_ids * n_tp + tp_index) // expert_span
    targets = dest_expert * CAP + lax.broadcasted_iota(jnp.int32, (n_grp, CAP), 1)
    outgoing_rows = []
    mixings = []
    for micro in range(NMB):
        start = micro * rows_mb
        selector, mixing = mixing_tables(
            chosen[start : start + rows_mb], weight[start : start + rows_mb], targets, experts, CAP
        )
        packed = jnp.dot(
            selector, moe_in[start : start + rows_mb], preferred_element_type=jnp.float32
        ).astype(jnp.bfloat16)
        packed = packed.reshape(n_grp, CAP, model_width)
        outgoing_rows.append(jnp.where(is_attn, packed, jnp.zeros_like(packed)))
        mixings.append(mixing)
    moe_parts = []
    for micro in range(NMB):
        empty_part = jnp.zeros_like(outgoing_rows[micro])
        sending = jnp.concatenate([empty_part, outgoing_rows[micro]], axis=0)
        arrived = lax.all_to_all(sending, ("side", "grp"), split_axis=0, concat_axis=0, tiled=True)[
            :n_grp
        ]
        flat_rows = arrived.reshape(-1, model_width)

        def compute_rows(flat_in):
            gate_val = jnp.dot(flat_in, gate_w[0], preferred_element_type=jnp.float32)
            up_val = jnp.dot(flat_in, up_w[0], preferred_element_type=jnp.float32)
            hidden = (jax.nn.silu(gate_val) * up_val).astype(jnp.bfloat16)
            return jnp.dot(hidden, down_w[0], preferred_element_type=jnp.float32).astype(
                jnp.bfloat16
            )

        def skip_rows(flat_in):
            return jnp.zeros_like(flat_in)

        answer = lax.cond(is_attn, skip_rows, compute_rows, flat_rows).reshape(arrived.shape)
        backward = jnp.concatenate([answer, jnp.zeros_like(answer)], axis=0)
        arrived_back = lax.all_to_all(
            backward, ("side", "grp"), split_axis=0, concat_axis=0, tiled=True
        )
        moe_parts.append(
            jnp.dot(
                mixings[micro],
                arrived_back[n_grp:].reshape(-1, model_width),
                preferred_element_type=jnp.float32,
            )
        )
    resid_parts = []
    latent_parts = []
    rope_parts = []
    attn_parts = []
    for micro in range(NMB):
        start = micro * rows_mb
        moe_total = lax.psum(moe_parts[micro].astype(jnp.bfloat16), "tp").astype(jnp.float32)
        updated = (x_rows[start : start + rows_mb] + moe_total).astype(jnp.bfloat16)
        updated_half = lax.dynamic_slice_in_dim(
            updated, tp_index * half_width, half_width, 1
        ).astype(jnp.float32)
        scaled = (updated_half * attn_gain[0].astype(jnp.float32)).astype(jnp.bfloat16)
        square_sums = jnp.sum(updated_half * updated_half, axis=1)
        partial_kv = lax.dot_general(
            scaled, kv_proj[0], (((1,), (1,)), ((), ())), preferred_element_type=jnp.float32
        )
        square_sums, kv_raw = lax.psum((square_sums, partial_kv), "tp")
        kv_raw = kv_raw * lax.rsqrt(square_sums / model_width + NORM_EPS)[:, None]
        latent = kv_raw[:, :latent_width]
        fresh_lat = (latent * rms_scale(latent) * kv_gain[0].astype(jnp.float32)).astype(
            jnp.bfloat16
        )
        seq_lengths = lengths[0, start : start + rows_mb]
        fresh_rot = rotate(kv_raw[:, latent_width:], seq_lengths).astype(jnp.bfloat16)
        operands = (
            query_latent[0, start : start + rows_mb],
            query_rope[0, start : start + rows_mb],
            cache_latent[0, start : start + rows_mb],
            cache_rope[0, start : start + rows_mb],
            seq_lengths,
            fresh_lat,
            fresh_rot,
        )

        def skip_attention(unused):
            return jnp.zeros((rows_mb, heads_here, latent_width), jnp.bfloat16)

        attended = lax.cond(is_attn, attend, skip_attention, operands)
        resid_parts.append(updated)
        latent_parts.append(fresh_lat)
        rope_parts.append(fresh_rot)
        attn_parts.append(attended)

    def keep_role(value):
        return jnp.where(is_attn, value, jnp.zeros_like(value))[None]

    return (
        keep_role(jnp.concatenate(resid_parts, axis=0)),
        keep_role(jnp.concatenate(latent_parts, axis=0)),
        keep_role(jnp.concatenate(rope_parts, axis=0)),
        keep_role(jnp.concatenate(attn_parts, axis=0)),
    )


def solution(mesh):
    in_specs = (
        P("side", "grp", None),
        P("side", None),
        P("side", None, None),
        P("side", "grp", None),
        P("side", None, ("grp", "tp")),
        P("side", None, ("grp", "tp")),
        P("side", ("grp", "tp"), None),
        P("side", "tp"),
        P("side", None, "tp"),
        P("side", None),
        P("side", "grp", None, None),
        P("side", "grp", None, None),
        P("side", "grp"),
        P("side", "grp", "tp", None),
        P("side", "grp", "tp"),
    )
    out_specs = (
        P("side", "grp", None),
        P("side", "grp", None),
        P("side", "grp", None),
        P("side", "grp", "tp", None),
    )
    return jax.shard_map(body, mesh=mesh, in_specs=in_specs, out_specs=out_specs, check_vma=False)
```

profile of v0, /device:TPU:1, one launch (start us, length us, event | category | flops | bytes accessed | tf_op | source)
XLA Modules:
  0.0 256.6 jit_solution(15487948896691143558)
XLA Ops:
  9.1 1.5 fusion.167
  14.2 1.4 concatenate.92
  15.6 7.4 %all-to-all-start = ((bf16[16,5,7168]{2,1,0:T(8,128)(2,1)}), bf16[16,5,7168]{2,1,0:T(8,128)(2,1)S(1)}, u32[]{:S(2)}, u32[]{:S(2)}) async-start(bf16[16,5,7168]{2,1,0:T(8,128)(2,1)} %concatenate.92), calls=%async_computation | async-start | bytes 3670016 | tf_op jit(solution)/shard_map/all_to_all | solution.py:141
  23.6 1.5 concatenate.95
  25.1 39.0 %all-to-all-done = bf16[16,5,7168]{2,1,0:T(8,128)(2,1)S(1)} async-done(((bf16[16,5,7168]{2,1,0:T(8,128)(2,1)}), bf16[16,5,7168]{2,1,0:T(8,128)(2,1)S(1)}, u32[]{:S(2)}, u32[]{:S(2)}) %all-to-all-start) | async-done | bytes 1146912 | tf_op jit(solution)/shard_map/all_to_all | solution.py:141
  65.3 5.3 %all-to-all-start.2 = ((bf16[16,5,7168]{2,1,0:T(8,128)(2,1)}), bf16[16,5,7168]{2,1,0:T(8,128)(2,1)S(1)}, u32[]{:S(2)}, u32[]{:S(2)}) async-start(bf16[16,5,7168]{2,1,0:T(8,128)(2,1)} %concatenate.95), calls=%async_computation.2 | async-start | bytes 3670016 | tf_op jit(solution)/shard_map/all_to_all | solution.py:141
  71.6 1.3 reshape.340
  72.9 1.4 concatenate.93
  74.3 37.5 %all-to-all-done.2 = bf16[16,5,7168]{2,1,0:T(8,128)(2,1)S(1)} async-done(((bf16[16,5,7168]{2,1,0:T(8,128)(2,1)}), bf16[16,5,7168]{2,1,0:T(8,128)(2,1)S(1)}, u32[]{:S(2)}, u32[]{:S(2)}) %all-to-all-start.2) | async-done | bytes 1146912 | tf_op jit(solution)/shard_map/all_to_all | solution.py:141
  113.1 5.4 %all-to-all-start.1 = ((bf16[16,5,7168]{2,1,0:T(8,128)(2,1)}), bf16[16,5,7168]{2,1,0:T(8,128)(2,1)S(1)}, u32[]{:S(2)}, u32[]{:S(2)}) async-start(bf16[16,5,7168]{2,1,0:T(8,128)(2,1)} %concatenate.93), calls=%async_computation.1 | async-start | bytes 3670016 | tf_op jit(solution)/shard_map/all_to_all | solution.py:159
  119.6 1.4 reshape.343
  121.0 1.5 concatenate.96
  122.4 37.1 %all-to-all-done.1 = bf16[16,5,7168]{2,1,0:T(8,128)(2,1)S(1)} async-done(((bf16[16,5,7168]{2,1,0:T(8,128)(2,1)}), bf16[16,5,7168]{2,1,0:T(8,128)(2,1)S(1)}, u32[]{:S(2)}, u32[]{:S(2)}) %all-to-all-start.1) | async-done | bytes 1146912 | tf_op jit(solution)/shard_map/all_to_all | solution.py:159
  159.6 5.4 %all-to-all-start.3 = ((bf16[16,5,7168]{2,1,0:T(8,128)(2,1)}), bf16[16,5,7168]{2,1,0:T(8,128)(2,1)}, u32[]{:S(2)}, u32[]{:S(2)}) async-start(bf16[16,5,7168]{2,1,0:T(8,128)(2,1)} %concatenate.96), calls=%async_computation.3 | async-start | bytes 3670016 | tf_op jit(solution)/shard_map/all_to_all | solution.py:159
  168.3 37.9 %all-to-all-done.3 = bf16[16,5,7168]{2,1,0:T(8,128)(2,1)} async-done(((bf16[16,5,7168]{2,1,0:T(8,128)(2,1)}), bf16[16,5,7168]{2,1,0:T(8,128)(2,1)}, u32[]{:S(2)}, u32[]{:S(2)}) %all-to-all-start.3) | async-done | bytes 1146912 | tf_op jit(solution)/shard_map/all_to_all | solution.py:159
  208.7 19.0 %all-reduce.8.cloned.1.call-done = (bf16[8,7168]{1,0:T(8,128)(2,1)}, bf16[8,7168]{1,0:T(8,128)(2,1)}) async-done(((bf16[8,7168]{1,0:T(8,128)(2,1)}, bf16[8,7168]{1,0:T(8,128)(2,1)}), (bf16[8,7168]{1,0:T(8,128)(2,1)}, bf16[8,7168]{1,0:T(8,128)(2,1)})) %all-reduce.8.cloned.1.call-update) | async-done | bytes 229392 | tf_op jit(solution)/shard_map/psum | solution.py:175
  229.1 3.4 %fusion.110 = f32[8,576]{1,0:T(8,128)S(1)} fusion(bf16[1,576,3584]{2,1,0:T(8,128)(2,1)} %param.31, f32[3584]{0:T(1024)S(1)} %convert_reduce_fusion.2, bf16[8,7168]{1,0:T(8,128)(2,1)S(1)} %get-tuple-element.120, s32[]{:T(128)S(6)} %select_n.113), kind=kOutput, calls=%fused_computation.114 | convolution fusion | flops 33116160 | bytes 4220932 | tf_op jit(solution)/shard_map/dot_general | solution.py:182
  233.9 3.6 %all-reduce.4 = (f32[8,576]{1,0:T(8,128)S(1)}, f32[8]{0:T(128)S(1)}, f32[8,576]{1,0:T(8,128)S(1)}, f32[8]{0:T(128)S(1)}) all-reduce(f32[8,576]{1,0:T(8,128)S(1)} %fusion.108, f32[8]{0:T(128)S(1)} %fusion.138, f32[8,576]{1,0:T(8,128)S(1)} %fusion.110, f32[8]{0:T(128)S(1)} %fusion.136), channel_id=1, replica_groups=mesh['side'=2,'grp'=8,'tp'=2] {'tp'}, use_global_device_ids=true, to_apply=%region_21.22 | all-reduce | flops 9232 | bytes 73856 | tf_op jit(solution)/shard_map/psum | solution.py:185
  238.5 4.2 %conditional.6 = (bf16[1,8,32,512]{3,2,1,0:T(8,128)(2,1)S(1)}) conditional(s32[]{:T(128)} %convert_element_type.178, () %tuple.40, (s32[1,8]{1,0:T(1,128)S(1)}, bf16[1,16,32,512]{3,2,1,0:T(8,128)(2,1)S(1)}, bf16[1,16,128,512]{3,2,1,0:T(8,128)(2,1)}, bf16[1,16,2048]{2,1,0:T(8,128)(2,1)S(1)}, bf16[1,16,64,128]{3,2,1,0:T(8,128)(2,1)S(1)}, ...), branch_computations={%region_25.26_spmd, %region_26.29_spmd} | conditional | flops 72456448 | bytes 3968584 | solution.py:206
  238.5 1.7 fusion.53
  241.2 1.6 fusion.49
  242.8 4.2 %conditional.7 = (bf16[1,8,32,512]{3,2,1,0:T(8,128)(2,1)S(1)}) conditional(s32[]{:T(128)} %convert_element_type.178, () %tuple.42, (s32[1,8]{1,0:T(1,128)S(1)}, bf16[1,16,32,512]{3,2,1,0:T(8,128)(2,1)S(1)}, bf16[1,16,128,512]{3,2,1,0:T(8,128)(2,1)}, bf16[1,16,2048]{2,1,0:T(8,128)(2,1)S(1)}, bf16[1,16,64,128]{3,2,1,0:T(8,128)(2,1)S(1)}, ...), branch_computations={%region_29.30_spmd, %region_30.33_spmd} | conditional | flops 72456448 | bytes 3968584 | solution.py:206
  242.8 1.7 fusion.81
  245.4 1.6 fusion.77
  (126 shorter events, 24.5 us)
Async XLA Ops:
  7.2 158.0 %copy-start = (bf16[1,16,7168]{2,1,0:T(8,128)(2,1)S(1)}, bf16[1,16,7168]{2,1,0:T(8,128)(2,1)}, u32[]{:S(2)}) copy-start(bf16[1,16,7168]{2,1,0:T(8,128)(2,1)} %param.25) | copy-start | bytes 688132
  11.4 2.2 copy-start.8
  12.5 3.1 %copy-start.17 = (f32[16]{0:T(128)}, f32[16]{0:T(128)S(1)}, u32[]{:S(2)}) copy-start(f32[16]{0:T(128)S(1)} %add_rsqrt_fusion.4) | copy-start | bytes 196
  15.6 48.5 %all-to-all-start = ((bf16[16,5,7168]{2,1,0:T(8,128)(2,1)}), bf16[16,5,7168]{2,1,0:T(8,128)(2,1)S(1)}, u32[]{:S(2)}, u32[]{:S(2)}) async-start(bf16[16,5,7168]{2,1,0:T(8,128)(2,1)} %concatenate.92), calls=%async_computation | async-start | bytes 3670016 | tf_op jit(solution)/shard_map/all_to_all | solution.py:141
  64.1 1.2 copy-start.3
  65.3 46.5 %all-to-all-start.2 = ((bf16[16,5,7168]{2,1,0:T(8,128)(2,1)}), bf16[16,5,7168]{2,1,0:T(8,128)(2,1)S(1)}, u32[]{:S(2)}, u32[]{:S(2)}) async-start(bf16[16,5,7168]{2,1,0:T(8,128)(2,1)} %concatenate.95), calls=%async_computation.2 | async-start | bytes 3670016 | tf_op jit(solution)/shard_map/all_to_all | solution.py:141
  70.8 0.8 copy-start.4
  111.8 1.3 copy-start.2
  113.1 46.5 %all-to-all-start.1 = ((bf16[16,5,7168]{2,1,0:T(8,128)(2,1)}), bf16[16,5,7168]{2,1,0:T(8,128)(2,1)S(1)}, u32[]{:S(2)}, u32[]{:S(2)}) async-start(bf16[16,5,7168]{2,1,0:T(8,128)(2,1)} %concatenate.93), calls=%async_computation.1 | async-start | bytes 3670016 | tf_op jit(solution)/shard_map/all_to_all | solution.py:159
  119.5 45.5 %copy-start.13 = (s32[1,16,8]{1,2,0:T(8,128)S(1)}, s32[1,16,8]{1,2,0:T(8,128)}, u32[]{:S(2)}) copy-start(s32[1,16,8]{1,2,0:T(8,128)} %param.26) | copy-start | bytes 1540
  119.5 45.6 %copy-start.14 = (bf16[1,3584]{1,0:T(2,128)(2,1)S(1)}, bf16[1,3584]{1,0:T(2,128)(2,1)}, u32[]{:S(2)}) copy-start(bf16[1,3584]{1,0:T(2,128)(2,1)} %param.30) | copy-start | bytes 21508
  119.5 45.7 %copy-start.6 = (bf16[1,16,7168]{2,1,0:T(8,128)(2,1)S(1)}, bf16[1,16,7168]{2,1,0:T(8,128)(2,1)}, u32[]{:S(2)}) copy-start(bf16[1,16,7168]{2,1,0:T(8,128)(2,1)} %param.23) | copy-start | bytes 688132
  119.5 45.7 %copy-start.9 = (f32[1,7168]{1,0:T(1,128)S(1)}, f32[1,7168]{1,0:T(1,128)}, u32[]{:S(2)}) copy-start(f32[1,7168]{1,0:T(1,128)} %copy-done.8) | copy-start | bytes 86020
  119.5 45.7 %copy-start.18 = (f32[16]{0:T(128)S(1)}, f32[16]{0:T(128)}, u32[]{:S(2)}) copy-start(f32[16]{0:T(128)} %copy-done.17) | copy-start | bytes 196
  119.6 46.6 %copy-start.12 = (pred[8,5,8,8]{3,2,1,0:T(8,128)(4,1)S(1)}, pred[8,5,8,8]{3,2,1,0:T(8,128)(4,1)}, u32[]{:S(2)}) copy-start(pred[8,5,8,8]{3,2,1,0:T(8,128)(4,1)} %get-tuple-element.126) | copy-start | bytes 7684
  119.6 47.1 %copy-start.11 = (pred[8,5,8,8]{3,2,1,0:T(8,128)(4,1)S(1)}, pred[8,5,8,8]{3,2,1,0:T(8,128)(4,1)}, u32[]{:S(2)}) copy-start(pred[8,5,8,8]{3,2,1,0:T(8,128)(4,1)} %get-tuple-element.127) | copy-start | bytes 7684
  159.6 46.6 %all-to-all-start.3 = ((bf16[16,5,7168]{2,1,0:T(8,128)(2,1)}), bf16[16,5,7168]{2,1,0:T(8,128)(2,1)}, u32[]{:S(2)}, u32[]{:S(2)}) async-start(bf16[16,5,7168]{2,1,0:T(8,128)(2,1)} %concatenate.96), calls=%async_computation.3 | async-start | bytes 3670016 | tf_op jit(solution)/shard_map/all_to_all | solution.py:159
  165.0 43.6 %copy-start.16 = (bf16[1,512]{1,0:T(2,128)(2,1)S(1)}, bf16[1,512]{1,0:T(2,128)(2,1)}, u32[]{:S(2)}) copy-start(bf16[1,512]{1,0:T(2,128)(2,1)} %param.32) | copy-start | bytes 3076
  165.0 43.7 %copy-start.15 = (s32[1,16]{1,0:T(1,128)S(1)}, s32[1,16]{1,0:T(1,128)}, u32[]{:S(2)}) copy-start(s32[1,16]{1,0:T(1,128)} %param.35) | copy-start | bytes 196
  165.0 62.8 %all-reduce.8.cloned.1.call-start = ((), (), s32[]{:S(2)}) async-start(), calls=%async_computation.4 | async-start | bytes 458752 | tf_op jit(solution)/shard_map/psum | solution.py:175
  227.8 4.7 %copy-start.1 = (bf16[1,576,3584]{2,1,0:T(8,128)(2,1)S(1)}, bf16[1,576,3584]{2,1,0:T(8,128)(2,1)}, u32[]{:S(2)}) copy-start(bf16[1,576,3584]{2,1,0:T(8,128)(2,1)} %param.31) | copy-start | bytes 12386308
  229.1 9.4 %copy-start.7 = (bf16[1,16,64,128]{3,2,1,0:T(8,128)(2,1)S(1)}, bf16[1,16,64,128]{3,2,1,0:T(8,128)(2,1)}, u32[]{:S(2)}) copy-start(bf16[1,16,64,128]{3,2,1,0:T(8,128)(2,1)} %param.34) | copy-start | bytes 786436
  229.1 9.4 %copy-start.10 = (bf16[1,16,2048]{2,1,0:T(8,128)(2,1)S(1)}, bf16[1,16,2048]{2,1,0:T(8,128)(2,1)}, u32[]{:S(2)}) copy-start(bf16[1,16,2048]{2,1,0:T(8,128)(2,1)} %param.37) | copy-start | bytes 196612
  229.1 9.4 %copy-start.19 = (bf16[1,16,32,512]{3,2,1,0:T(8,128)(2,1)S(1)}, bf16[1,16,32,512]{3,2,1,0:T(8,128)(2,1)}, u32[]{:S(2)}) copy-start(bf16[1,16,32,512]{3,2,1,0:T(8,128)(2,1)} %param.36) | copy-start | bytes 1572868
  (1 other events, 0.8 us)
Sparse Core Ops, SparseCore 0:
  208.7 19.0 all-reduce.7
where the time goes:
time: 258 us; the launch traced here: 257 us
  waiting for transfers between devices  171 us (66%)
  starting transfers between devices  23.6 us (9%)
  matrix products  16.4 us (6%)
  local copies, waits for them, and re-layouts  16 us (6%)
  between operations  14.5 us (6%)
  other arithmetic  11.6 us (4%)
  blocking collectives  3.63 us (1%)
    all_to_all x2, waiting for transfers between devices, body(): lax.all_to_all(sending, ('side', 'grp'), split_axis=0, concat_axis=0, til...  76.5 us
    all_to_all x2, waiting for transfers between devices, body(): lax.all_to_all(backward, ('side', 'grp'), split_axis=0, concat_axis=0, ti...  75 us
    psum x1, waiting for transfers between devices, body(): lax.psum(moe_parts[micro].astype(jnp.bfloat16), 'tp').astype(jnp.float32)  19 us
    all_to_all x2, starting transfers between devices, body(): lax.all_to_all(sending, ('side', 'grp'), split_axis=0, concat_axis=0, til...  12.8 us
    all_to_all x2, starting transfers between devices, body(): lax.all_to_all(backward, ('side', 'grp'), split_axis=0, concat_axis=0, ti...  10.8 us
  transfers between devices with their start and end apart: 5, of which 5 were waited for; matrix products, arithmetic and copies ran while one was open for 4% of the time, Pallas kernels for 0%

commit v1 on v0

v1 whole, which is shorter than its diff:
```python
import functools
import math

import jax
import jax.numpy as jnp
from jax import lax
from jax.experimental import pallas as pl
from jax.experimental.pallas import tpu as pltpu
from jax.sharding import PartitionSpec as P

NORM_EPS = 1e-06
ROUTE_SCALE = 2.5
ROPE_BASE = 10000.0
SCORE_SCALE = 192.0 ** (-0.5)
MESH = pl.DeviceIdType.MESH
CHUNKS = 4
NT = (((1,), (1,)), ((), ()))


def kernel(
    n_grp, n_tp, res_ref, gain_ref, router_ref, routes_ref, again_ref, kvgain_ref, len_ref,
    qrope_ref, gate_ref, up_ref, down_ref, kvp_ref, cache_ref, crope_ref, qlat_ref,
    resid_ref, nlat_ref, nrope_ref, attn_ref,
    msg, xb, wg, wu, wd, acc_g, acc_u, hid, pown, pother, r0, sx, r1, tbuf, ra, hs, hr,
    kvs, kvr, kvw, cl, cr, ql, o_acc, m_acc, l_acc,
    load_sem, d_send, d_recv, f_send, x_send, x_recv, c_send, c_recv, z_send, z_recv, h_send, h_recv, k_sem,
):
    side = lax.axis_index("side")
    grp = lax.axis_index("grp")
    tp = lax.axis_index("tp")
    n_a = n_grp // 2
    a = grp // 2
    b = grp % 2
    rows, width = res_ref.shape
    half = width // 2
    cw = half // CHUNKS
    experts = router_ref.shape[0]
    ff = gate_ref.shape[2]
    lat = kvgain_ref.shape[1]
    rope = crope_ref.shape[2]
    kvwid = lat + rope
    core_peer = (side, grp, 1 - tp)
    x_peer = (side, a * 2 + 1 - b, tp)

    def line(other_side, where):
        return (other_side, where * 2 + b, tp)

    def remote(src, dst, ssem, rsem, dev):
        return pltpu.make_async_remote_copy(
            src_ref=src, dst_ref=dst, send_sem=ssem, recv_sem=rsem, device_id=dev, device_id_type=MESH
        )

    def block(ref, which, pos):
        return ref.at[which, pl.ds(pl.multiple_of(pos * rows, rows), rows), :]

    barrier = pltpu.get_barrier_semaphore()

    def greet():
        pl.semaphore_signal(barrier, inc=1, device_id=core_peer, device_id_type=MESH)
        for i in range(n_a):
            pl.semaphore_signal(barrier, inc=1, device_id=line(1 - side, i), device_id_type=MESH)

    @pl.when(side == 1)
    def _():
        own = pl.multiple_of(tp * half, 128)
        oth = pl.multiple_of((1 - tp) * half, 128)
        loads = []
        for i, at in enumerate((own, oth)):
            loads.append(pltpu.make_async_copy(gate_ref.at[0, pl.ds(at, half), :], wg.at[i], load_sem.at[i]))
            loads.append(pltpu.make_async_copy(up_ref.at[0, pl.ds(at, half), :], wu.at[i], load_sem.at[2 + i]))
        for i, at in enumerate((own, oth)):
            loads.append(pltpu.make_async_copy(down_ref.at[0, :, pl.ds(at, half)], wd.at[i], load_sem.at[4 + i]))
        for ld in loads:
            ld.start()
        greet()
        pl.semaphore_signal(barrier, inc=1, device_id=x_peer, device_id_type=MESH)
        pl.semaphore_wait(barrier, n_a + 2)

        sends = []
        for d in range(n_a):
            src_a = lax.rem(a - d + n_a, n_a)
            pos = b * n_a + src_a
            here = block(xb, 0, pos)
            remote(here, here, f_send.at[0, d], d_recv.at[0, pos], core_peer).wait_recv()
            fwd = remote(here, here, x_send.at[d], d_recv.at[0, pos], x_peer)
            fwd.start()
            cfwd = remote(here, block(xb, 1, pos), f_send.at[0, d], d_recv.at[1, pos], core_peer)
            cfwd.start()
            sends += [fwd, cfwd]
        for d in range(n_a):
            src_a = lax.rem(a - d + n_a, n_a)
            pos = (1 - b) * n_a + src_a
            here = block(xb, 0, pos)
            remote(here, here, f_send.at[1, d], d_recv.at[0, pos], core_peer).wait_recv()
            cfwd = remote(here, block(xb, 1, pos), f_send.at[1, d], d_recv.at[1, pos], core_peer)
            cfwd.start()
            sends.append(cfwd)

        tn = min(256, ff)
        loads[0].wait()
        loads[1].wait()

        @pl.loop(0, ff // tn)
        def _(n):
            cols = pl.ds(pl.multiple_of(n * tn, tn), tn)
            x0 = xb[0, :, :half]
            acc_g[:, cols] = jnp.dot(x0, wg[0, :, cols], preferred_element_type=jnp.float32)
            acc_u[:, cols] = jnp.dot(x0, wu[0, :, cols], preferred_element_type=jnp.float32)

        for pos in range(n_grp):
            here = block(xb, 1, pos)
            remote(here, here, f_send.at[0, 0], d_recv.at[1, pos], core_peer).wait_recv()
        loads[2].wait()
        loads[3].wait()

        @pl.loop(0, ff // tn)
        def _(n):
            cols = pl.ds(pl.multiple_of(n * tn, tn), tn)
            x1 = xb[1, :, :half]
            g = acc_g[:, cols] + jnp.dot(x1, wg[1, :, cols], preferred_element_type=jnp.float32)
            u = acc_u[:, cols] + jnp.dot(x1, wu[1, :, cols], preferred_element_type=jnp.float32)
            hid[:, cols] = (g / (1.0 + jnp.exp(-g)) * u).astype(jnp.bfloat16)

        loads[4].wait()
        loads[5].wait()
        span = n_grp * n_tp // experts
        expert = (grp * n_tp + tp) // span
        table = xb[0, :, half:].astype(jnp.float32)
        lanes = lax.broadcasted_iota(jnp.int32, table.shape, 1)
        weight = jnp.sum(jnp.where(lanes == expert, table, 0.0), axis=1, keepdims=True)
        half_rows = n_a * rows
        mine = pl.ds(pl.multiple_of(b * half_rows, rows), half_rows)
        theirs = pl.ds(pl.multiple_of((1 - b) * half_rows, rows), half_rows)

        def down(j):
            h = hid[...]
            cols = slice(j * cw, (j + 1) * cw)
            p1 = jnp.dot(h, wd[1, :, cols], preferred_element_type=jnp.float32)
            pother[j] = (p1 * weight).astype(jnp.bfloat16)
            cp = remote(pother.at[j], r0.at[j], c_send.at[j], c_recv.at[j], core_peer)
            cp.start()
            p0 = jnp.dot(h, wd[0, :, cols], preferred_element_type=jnp.float32)
            pown[j] = (p0 * weight).astype(jnp.bfloat16)
            return cp

        def stage_x(j, cp):
            cp.wait_recv()
            sx[j] = (pown[j, theirs, :].astype(jnp.float32) + r0[j, theirs, :].astype(jnp.float32)).astype(jnp.bfloat16)
            xp = remote(sx.at[j], r1.at[j], x_send.at[n_a + j], x_recv.at[j], x_peer)
            xp.start()
            return xp

        def stage_z(j, xp):
            xp.wait_recv()
            tbuf[j] = (
                pown[j, mine, :].astype(jnp.float32)
                + r0[j, mine, :].astype(jnp.float32)
                + r1[j].astype(jnp.float32)
            ).astype(jnp.bfloat16)
            out = []
            for d in range(n_a):
                to_a = lax.rem(a + d, n_a)
                zp = remote(
                    block(tbuf, j, to_a), ra.at[j, a], z_send.at[j, d], z_recv.at[j, a], line(0, to_a)
                )
                zp.start()
                out.append(zp)
            return out

        cps, xps = [], []
        for j in range(CHUNKS):
            cps.append(down(j))
            if j >= 1:
                xps.append(stage_x(j - 1, cps[j - 1]))
        xps.append(stage_x(CHUNKS - 1, cps[-1]))
        for j in range(CHUNKS):
            sends += stage_z(j, xps[j])
        resid_ref[...] = jnp.zeros_like(resid_ref)
        nlat_ref[...] = jnp.zeros_like(nlat_ref)
        nrope_ref[...] = jnp.zeros_like(nrope_ref)
        attn_ref[...] = jnp.zeros_like(attn_ref)
        for cp in sends + cps + xps:
            cp.wait_send()

    @pl.when(side == 0)
    def _():
        loads = [
            pltpu.make_async_copy(qlat_ref.at[0], ql, load_sem.at[0]),
            pltpu.make_async_copy(cache_ref.at[0], cl, load_sem.at[1]),
            pltpu.make_async_copy(crope_ref.at[0], cr, load_sem.at[2]),
            pltpu.make_async_copy(kvp_ref.at[0], kvw, load_sem.at[3]),
        ]
        for ld in loads:
            ld.start()
        greet()
        x = res_ref[...].astype(jnp.float32)
        scale = lax.rsqrt(jnp.mean(x * x, axis=1, keepdims=True) + NORM_EPS)
        normed = x * scale * gain_ref[...].astype(jnp.float32)
        logits = lax.dot_general(
            normed, router_ref[...].astype(jnp.float32), NT,
            precision=lax.Precision.HIGHEST, preferred_element_type=jnp.float32,
        )
        s = 1.0 / (1.0 + jnp.exp(-logits))
        ids = lax.broadcasted_iota(jnp.int32, s.shape, 1)
        chosen = jnp.zeros(s.shape, jnp.float32)
        for k in range(routes_ref.shape[1]):
            chosen = jnp.where(routes_ref[:, k : k + 1] == ids, 1.0, chosen)
        picked = s * chosen
        dense = ROUTE_SCALE * picked / jnp.sum(picked, axis=1, keepdims=True)
        narrow = normed.astype(jnp.bfloat16)
        msg[:, :half] = jnp.where(tp == 0, narrow[:, :half], narrow[:, half:])
        msg[:, half:] = jnp.zeros((rows, 128), jnp.bfloat16)
        msg[:, half : half + experts] = dense.astype(jnp.bfloat16)
        pl.semaphore_wait(barrier, n_a + 1)
        pos = b * n_a + a
        sends = []
        for d in range(n_a):
            to_a = lax.rem(a + d, n_a)
            cp = remote(msg, block(xb, 0, pos), d_send.at[d], d_recv.at[0, pos], line(1, to_a))
            cp.start()
            sends.append(cp)

        for ld in loads:
            ld.wait()

        @pl.loop(0, rows)
        def _(t):
            sc = lax.dot_general(ql[t], cl[t], NT, preferred_element_type=jnp.float32)
            sc = sc + jnp.dot(qrope_ref[t], cr[t], preferred_element_type=jnp.float32)
            sc = sc * SCORE_SCALE
            usable = lax.broadcasted_iota(jnp.int32, sc.shape, 1) < len_ref[t]
            sc = jnp.where(usable, sc, -1e30)
            peak = jnp.max(sc, axis=1, keepdims=True)
            wts = jnp.where(usable, jnp.exp(sc - peak), 0.0)
            m_acc[t] = jnp.broadcast_to(peak, sc.shape)
            l_acc[t] = jnp.broadcast_to(jnp.sum(wts, axis=1, keepdims=True), sc.shape)
            o_acc[t] = jnp.dot(wts.astype(jnp.bfloat16), cl[t], preferred_element_type=jnp.float32)

        kv = jnp.zeros((rows, kvwid), jnp.float32)
        sq = jnp.zeros((rows, 1), jnp.float32)
        for j in range(CHUNKS):
            total = jnp.zeros((rows, cw), jnp.float32)
            for i in range(n_a):
                here = ra.at[j, i]
                remote(here, here, h_send.at[j], z_recv.at[j, i], core_peer).wait_recv()
                total = total + ra[j, i].astype(jnp.float32)
            cols = pl.ds(pl.multiple_of(tp * half + j * cw, 128), cw)
            h = (res_ref[:, cols].astype(jnp.float32) + total).astype(jnp.bfloat16)
            hs[j] = h
            cp = remote(hs.at[j], hr.at[j], h_send.at[j], h_recv.at[j], core_peer)
            cp.start()
            sends.append(cp)
            resid_ref[:, cols] = h
            hf = h.astype(jnp.float32)
            span = slice(j * cw, (j + 1) * cw)
            scaled = (hf * again_ref[:, span].astype(jnp.float32)).astype(jnp.bfloat16)
            kv = kv + lax.dot_general(scaled, kvw[:, span], NT, preferred_element_type=jnp.float32)
            sq = sq + jnp.sum(hf * hf, axis=1, keepdims=True)
        kvs[:, :kvwid] = kv
        kvs[:, kvwid:] = jnp.broadcast_to(sq, (rows, kvs.shape[1] - kvwid))
        cp = remote(kvs, kvr, k_sem.at[0], k_sem.at[1], core_peer)
        cp.start()
        sends.append(cp)
        cp.wait_recv()
        both = kvs[...] + kvr[...]
        norm = lax.rsqrt(both[:, kvwid : kvwid + 1] / width + NORM_EPS)
        latent = both[:, :lat] * norm
        lscale = lax.rsqrt(jnp.mean(latent * latent, axis=1, keepdims=True) + NORM_EPS)
        fresh = (latent * lscale * kvgain_ref[...].astype(jnp.float32)).astype(jnp.bfloat16)
        nlat_ref[...] = fresh
        rot = both[:, lat:] * norm
        lane = lax.broadcasted_iota(jnp.int32, rot.shape, 1)
        step = jnp.where(lane < rope // 2, lane, lane - rope // 2).astype(jnp.float32)
        freq = jnp.exp(-(2.0 * step / rope) * math.log(ROPE_BASE))
        row_id = lax.broadcasted_iota(jnp.int32, rot.shape, 0)
        position = jnp.zeros(rot.shape, jnp.float32)
        for t in range(rows):
            position = jnp.where(row_id == t, len_ref[t].astype(jnp.float32), position)
        angle = position * freq
        up_part = pltpu.roll(rot, 128 - rope // 2, 1)
        down_part = pltpu.roll(rot, rope // 2, 1)
        turned = rot * jnp.cos(angle) + jnp.where(lane < rope // 2, -up_part, down_part) * jnp.sin(angle)
        turned = turned[:, :rope].astype(jnp.bfloat16)
        nrope_ref[...] = turned
        fresh_f = fresh.astype(jnp.float32)
        turned_f = turned.astype(jnp.float32)
        for t in range(rows):
            fl = fresh_f[t : t + 1]
            own = jnp.sum(ql[t].astype(jnp.float32) * fl, axis=1, keepdims=True)
            own = own + jnp.sum(qrope_ref[t].astype(jnp.float32) * turned_f[t : t + 1], axis=1, keepdims=True)
            own = own * SCORE_SCALE
            m_old = m_acc[t, :, :1]
            peak = jnp.maximum(m_old, own)
            keep = jnp.exp(m_old - peak)
            ow = jnp.exp(own - peak)
            inv = 1.0 / (l_acc[t, :, :1] * keep + ow)
            attn_ref[t] = (o_acc[t] * (keep * inv) + (ow * inv) * fl).astype(jnp.bfloat16)
        for j in range(CHUNKS):
            here = hr.at[j]
            remote(here, here, h_send.at[j], h_recv.at[j], core_peer).wait_recv()
            cols = pl.ds(pl.multiple_of((1 - tp) * half + j * cw, 128), cw)
            resid_ref[:, cols] = hr[j]
        for cp in sends:
            cp.wait_send()


def body(
    residual, moe_gain, router, routes, gate_w, up_w, down_w, attn_gain, kv_proj, kv_gain,
    cache_latent, cache_rope, lengths, query_latent, query_rope,
):
    n_grp = lax.axis_size("grp")
    n_tp = lax.axis_size("tp")
    n_a = n_grp // 2
    rows, width = residual.shape[1:]
    half = width // 2
    cw = half // CHUNKS
    ff = gate_w.shape[2]
    all_rows = n_grp * rows
    lat = kv_gain.shape[1]
    heads = query_latent.shape[2]
    slots = cache_latent.shape[2]
    rope = cache_rope.shape[2]
    bf, f32 = jnp.bfloat16, jnp.float32
    vmem, smem, hbm = (pl.BlockSpec(memory_space=s) for s in (pltpu.VMEM, pltpu.SMEM, pl.ANY))
    dma = pltpu.SemaphoreType.DMA
    q_rot = query_rope[0].reshape(rows, heads, rope)
    outs = pl.pallas_call(
        functools.partial(kernel, n_grp, n_tp),
        out_shape=(
            jax.ShapeDtypeStruct((rows, width), bf),
            jax.ShapeDtypeStruct((rows, lat), bf),
            jax.ShapeDtypeStruct((rows, rope), bf),
            jax.ShapeDtypeStruct((rows, heads, lat), bf),
        ),
        in_specs=[vmem] * 6 + [smem, vmem] + [hbm] * 7,
        out_specs=(vmem,) * 4,
        scratch_shapes=[
            pltpu.VMEM((rows, half + 128), bf),
            pltpu.VMEM((2, all_rows, half + 128), bf),
            pltpu.VMEM((2, half, ff), bf),
            pltpu.VMEM((2, half, ff), bf),
            pltpu.VMEM((2, ff, half), bf),
            pltpu.VMEM((all_rows, ff), f32),
            pltpu.VMEM((all_rows, ff), f32),
            pltpu.VMEM((all_rows, ff), bf),
            pltpu.VMEM((CHUNKS, all_rows, cw), bf),
            pltpu.VMEM((CHUNKS, all_rows, cw), bf),
            pltpu.VMEM((CHUNKS, all_rows, cw), bf),
            pltpu.VMEM((CHUNKS, n_a * rows, cw), bf),
            pltpu.VMEM((CHUNKS, n_a * rows, cw), bf),
            pltpu.VMEM((CHUNKS, n_a * rows, cw), bf),
            pltpu.VMEM((CHUNKS, n_a, rows, cw), bf),
            pltpu.VMEM((CHUNKS, rows, cw), bf),
            pltpu.VMEM((CHUNKS, rows, cw), bf),
            pltpu.VMEM((rows, lat + 128), f32),
            pltpu.VMEM((rows, lat + 128), f32),
            pltpu.VMEM(kv_proj.shape[1:], bf),
            pltpu.VMEM(cache_latent.shape[1:], bf),
            pltpu.VMEM(cache_rope.shape[1:], bf),
            pltpu.VMEM(query_latent.shape[1:], bf),
            pltpu.VMEM((rows, heads, lat), f32),
            pltpu.VMEM((rows, heads, slots), f32),
            pltpu.VMEM((rows, heads, slots), f32),
            dma((6,)),
            dma((n_a,)),
            dma((2, n_grp)),
            dma((2, n_a)),
            dma((n_a + CHUNKS,)),
            dma((CHUNKS,)),
            dma((CHUNKS,)),
            dma((CHUNKS,)),
            dma((CHUNKS, n_a)),
            dma((CHUNKS, n_a)),
            dma((CHUNKS,)),
            dma((CHUNKS,)),
            dma((2,)),
        ],
        compiler_params=pltpu.CompilerParams(
            collective_id=0, has_side_effects=True, vmem_limit_bytes=63 * 1024 * 1024
        ),
    )(
        residual[0], moe_gain, router[0], routes[0], attn_gain, kv_gain, lengths[0], q_rot,
        gate_w, up_w, down_w, kv_proj, cache_latent, cache_rope, query_latent,
    )
    return tuple(o[None] for o in outs)


def solution(mesh):
    in_specs = (
        P("side", "grp", None),
        P("side", None),
        P("side", None, None),
        P("side", "grp", None),
        P("side", None, ("grp", "tp")),
        P("side", None, ("grp", "tp")),
        P("side", ("grp", "tp"), None),
        P("side", "tp"),
        P("side", None, "tp"),
        P("side", None),
        P("side", "grp", None, None),
        P("side", "grp", None, None),
        P("side", "grp"),
        P("side", "grp", "tp", None),
        P("side", "grp", "tp"),
    )
    out_specs = (
        P("side", "grp", None),
        P("side", "grp", None),
        P("side", "grp", None),
        P("side", "grp", "tp", None),
    )
    return jax.shard_map(body, mesh=mesh, in_specs=in_specs, out_specs=out_specs, check_vma=False)
```

time: 258 us -> 66.9 us (0.26)
  waiting for transfers between devices: 171 us -> 0 us
  Pallas kernels: 0 us -> 56.7 us
  starting transfers between devices: 23.6 us -> 0 us
  matrix products: 16.4 us -> 0 us
  between operations: 14.5 us -> 0.64 us
  other arithmetic: 11.6 us -> 0 us
  local copies, waits for them, and re-layouts: 16 us -> 9.16 us
  blocking collectives: 3.63 us -> 0 us
    all_to_all x4 -> x0, waiting for transfers between devices: 152 us -> none  [the longest x2 76.5 us: body(): lax.all_to_all(sending, ('side', 'grp'), split_axis=0, concat_axis=0, til...]
    pallas_call x0 -> x1, Pallas kernels: none -> 56.7 us  [body(): pl.pallas_call(functools.partial(kernel, n_grp, n_tp), out_shape=(jax.Sha...]
    all_to_all x4 -> x0, starting transfers between devices: 23.6 us -> none  [the longest x2 12.8 us: body(): lax.all_to_all(sending, ('side', 'grp'), split_axis=0, concat_axis=0, til...]
    psum x1 -> x0, waiting for transfers between devices: 19 us -> none  [body(): lax.psum(moe_parts[micro].astype(jnp.bfloat16), 'tp').astype(jnp.float32)]
    dot_general x19 -> x0, matrix products: 16.4 us -> none  [the longest x2 4.61 us: body(): lax.dot_general(scaled, kv_proj[0], (((1,), (1,)), ((), ())), preferred_e...]
    concatenate x4 -> x0, local copies, waits for them, and re-layouts: 5.76 us -> none  [the longest x2 2.88 us: body(): sending = jnp.concatenate([empty_part, outgoing_rows[micro]], axis=0)]
    psum x1 -> x0, blocking collectives: 3.63 us -> none  [body(): square_sums, kv_raw = lax.psum((square_sums, partial_kv), 'tp')]
    reduce_sum x12 -> x0, other arithmetic: 3.19 us -> none  [the longest x3 1.35 us: rms_scale(): jnp.mean(values * values, axis=-1, keepdims=True) + NORM_EPS]
  transfers between devices with their start and end apart: 5 -> 0, of which waited for: 5 -> 0; matrix products, arithmetic and copies ran while one was open for 4% -> 0% of each run, Pallas kernels for 0% -> 0%
where the time goes in v1:
time: 66.9 us; the launch traced here: 66.5 us
  Pallas kernels  56.7 us (85%)
  local copies, waits for them, and re-layouts  9.16 us (14%)
    pallas_call x1, Pallas kernels, body(): pl.pallas_call(functools.partial(kernel, n_grp, n_tp), out_shape=(jax.Sha...  56.7 us
    unnamed x4, local copies, waits for them, and re-layouts  6.11 us
    another operation x1, local copies, waits for them, and re-layouts, body(): q_rot = query_rope[0].reshape(rows, heads, rope)  1.69 us
    squeeze x1, local copies, waits for them, and re-layouts, body(): routes[0]  1.36 us

profile of v1, /device:TPU:1, one launch (start us, length us, event | category | flops | bytes accessed | tf_op | source)
XLA Modules:
  0.0 66.5 jit_solution(38034819182022473)
XLA Ops:
  0.6 1.4 %copy.19.routes_ref = s32[16,8]{1,0:T(8,128)} copy(s32[16,8]{0,1:T(8,128)} %bitcast.13) | data formatting | bytes 1024 | tf_op jit(solution)/shard_map/squeeze | solution.py:382
  2.0 1.7 %reshape_squeeze.3.qrope_ref = bf16[16,32,64]{2,1,0:T(8,128)(2,1)} reshape(bf16[1,16,2048]{2,1,0:T(8,128)(2,1)} %param.29) | data formatting | bytes 131072 | tf_op jit(solution)/shard_map/reshape;squeeze | solution.py:326
  3.7 56.7 %shard_map.174 = (bf16[16,7168]{1,0:T(8,128)(2,1)}, bf16[16,512]{1,0:T(8,128)(2,1)}, bf16[16,64]{1,0:T(8,128)(2,1)}, bf16[16,32,512]{2,1,0:T(8,128)(2,1)}) custom-call(bf16[16,7168]{1,0:T(8,128)(2,1)} %bitcast.10, bf16[1,7168]{1,0:T(2,128)(2,1)} %gain_ref.1, bf16[16,7168]{1,0:T(8,128)(2,1)} %bitcast.11, s32[16,8]{1,0:T(8,128)} %copy.19.routes_ref, ...), custom_call_target="tpu_custom_call" | custom-call | tf_op jit(solution)/shard_map/pallas_call | solution.py:327
  60.4 1.6 %copy.24 = bf16[1,16,7168]{2,1,0:T(8,128)(2,1)} copy(bf16[1,16,7168]{2,1,0:T(8,128)(2,1)} %bitcast.9) | data formatting | bytes 458752
  62.0 1.3 %copy.25 = bf16[1,16,512]{2,1,0:T(8,128)(2,1)} copy(bf16[1,16,512]{2,1,0:T(8,128)(2,1)} %bitcast.12) | data formatting | bytes 32768
  63.4 1.3 %copy.26 = bf16[1,16,64]{2,1,0:T(8,128)(2,1)} copy(bf16[1,16,64]{2,1,0:T(8,128)(2,1)} %bitcast.14) | data formatting | bytes 4096
  64.6 1.9 %copy.27 = bf16[1,16,32,512]{3,2,1,0:T(8,128)(2,1)} copy(bf16[1,16,32,512]{3,2,1,0:T(8,128)(2,1)} %bitcast.8) | data formatting | bytes 1048576

commit v2 on v1

--- a/solution.py
+++ b/solution.py
@@ -13,7 +13,8 @@
 ROPE_BASE = 10000.0
 SCORE_SCALE = 192.0 ** (-0.5)
 MESH = pl.DeviceIdType.MESH
-CHUNKS = 4
+CHUNKS = 7
+PIECES = 4
 NT = (((1,), (1,)), ((), ()))
 
 
@@ -22,8 +23,8 @@
     qrope_ref, gate_ref, up_ref, down_ref, kvp_ref, cache_ref, crope_ref, qlat_ref,
     resid_ref, nlat_ref, nrope_ref, attn_ref,
     msg, xb, wg, wu, wd, acc_g, acc_u, hid, pown, pother, r0, sx, r1, tbuf, ra, hs, hr,
-    kvs, kvr, kvw, cl, cr, ql, o_acc, m_acc, l_acc,
-    load_sem, d_send, d_recv, f_send, x_send, x_recv, c_send, c_recv, z_send, z_recv, h_send, h_recv, k_sem,
+    kvs, kvr, kvw, cl, cr, qr, ql, o_acc, m_acc, l_acc,
+    load_sem, d_send, d_recv, f_send, f_recv, x_send, y_send, x_recv, c_send, c_recv, z_send, z_recv, h_send, h_recv, k_sem,
 ):
     side = lax.axis_index("side")
     grp = lax.axis_index("grp")
@@ -34,6 +35,7 @@
     rows, width = res_ref.shape
     half = width // 2
     cw = half // CHUNKS
+    kc = half // PIECES
     experts = router_ref.shape[0]
     ff = gate_ref.shape[2]
     lat = kvgain_ref.shape[1]
@@ -50,8 +52,9 @@
             src_ref=src, dst_ref=dst, send_sem=ssem, recv_sem=rsem, device_id=dev, device_id_type=MESH
         )
 
-    def block(ref, which, pos):
-        return ref.at[which, pl.ds(pl.multiple_of(pos * rows, rows), rows), :]
+    def block(ref, which, k, pos):
+        at = pl.ds(pl.multiple_of(pos * rows, rows), rows)
+        return ref.at[which, k, at, :] if k == PIECES - 1 else ref.at[which, k, at, :kc]
 
     barrier = pltpu.get_barrier_semaphore()
 
@@ -65,11 +68,20 @@
         own = pl.multiple_of(tp * half, 128)
         oth = pl.multiple_of((1 - tp) * half, 128)
         loads = []
+        for k in range(PIECES):
+            piece = pl.ds(k * kc, kc)
+            for i, at in enumerate((own, oth)):
+                source = pl.ds(pl.multiple_of(at + k * kc, 128), kc)
+                for w_ref, w_vmem in ((gate_ref, wg), (up_ref, wu)):
+                    loads.append(
+                        pltpu.make_async_copy(
+                            w_ref.at[0, source, :], w_vmem.at[i, piece, :], load_sem.at[len(loads)]
+                        )
+                    )
         for i, at in enumerate((own, oth)):
-            loads.append(pltpu.make_async_copy(gate_ref.at[0, pl.ds(at, half), :], wg.at[i], load_sem.at[i]))
-            loads.append(pltpu.make_async_copy(up_ref.at[0, pl.ds(at, half), :], wu.at[i], load_sem.at[2 + i]))
-        for i, at in enumerate((own, oth)):
-            loads.append(pltpu.make_async_copy(down_ref.at[0, :, pl.ds(at, half)], wd.at[i], load_sem.at[4 + i]))
+            loads.append(
+                pltpu.make_async_copy(down_ref.at[0, :, pl.ds(at, half)], wd.at[i], load_sem.at[len(loads)])
+            )
         for ld in loads:
             ld.start()
         greet()
@@ -77,55 +89,63 @@
         pl.semaphore_wait(barrier, n_a + 2)
 
         sends = []
-        for d in range(n_a):
-            src_a = lax.rem(a - d + n_a, n_a)
-            pos = b * n_a + src_a
-            here = block(xb, 0, pos)
-            remote(here, here, f_send.at[0, d], d_recv.at[0, pos], core_peer).wait_recv()
-            fwd = remote(here, here, x_send.at[d], d_recv.at[0, pos], x_peer)
-            fwd.start()
-            cfwd = remote(here, block(xb, 1, pos), f_send.at[0, d], d_recv.at[1, pos], core_peer)
-            cfwd.start()
-            sends += [fwd, cfwd]
-        for d in range(n_a):
-            src_a = lax.rem(a - d + n_a, n_a)
-            pos = (1 - b) * n_a + src_a
-            here = block(xb, 0, pos)
-            remote(here, here, f_send.at[1, d], d_recv.at[0, pos], core_peer).wait_recv()
-            cfwd = remote(here, block(xb, 1, pos), f_send.at[1, d], d_recv.at[1, pos], core_peer)
-            cfwd.start()
-            sends.append(cfwd)
+
+        def direct(k):
+            for d in range(n_a):
+                pos = b * n_a + lax.rem(a - d + n_a, n_a)
+                here = block(xb, 0, k, pos)
+                remote(here, here, f_send.at[k], d_recv.at[k, pos], core_peer).wait_recv()
+                fwd = remote(here, here, x_send.at[k, d], d_recv.at[k, pos], x_peer)
+                fwd.start()
+                sends.append(fwd)
+
+        def across(k):
+            for d in range(n_a):
+                pos = (1 - b) * n_a + lax.rem(a - d + n_a, n_a)
+                here = block(xb, 0, k, pos)
+                remote(here, here, f_send.at[k], d_recv.at[k, pos], core_peer).wait_recv()
+            cp = remote(xb.at[0, k, :, :kc], xb.at[1, k, :, :kc], f_send.at[k], f_recv.at[k], core_peer)
+            cp.start()
+            sends.append(cp)
+            return cp
 
         tn = min(256, ff)
-        loads[0].wait()
-        loads[1].wait()
-
-        @pl.loop(0, ff // tn)
-        def _(n):
-            cols = pl.ds(pl.multiple_of(n * tn, tn), tn)
-            x0 = xb[0, :, :half]
-            acc_g[:, cols] = jnp.dot(x0, wg[0, :, cols], preferred_element_type=jnp.float32)
-            acc_u[:, cols] = jnp.dot(x0, wu[0, :, cols], preferred_element_type=jnp.float32)
-
-        for pos in range(n_grp):
-            here = block(xb, 1, pos)
-            remote(here, here, f_send.at[0, 0], d_recv.at[1, pos], core_peer).wait_recv()
-        loads[2].wait()
-        loads[3].wait()
-
-        @pl.loop(0, ff // tn)
-        def _(n):
-            cols = pl.ds(pl.multiple_of(n * tn, tn), tn)
-            x1 = xb[1, :, :half]
-            g = acc_g[:, cols] + jnp.dot(x1, wg[1, :, cols], preferred_element_type=jnp.float32)
-            u = acc_u[:, cols] + jnp.dot(x1, wu[1, :, cols], preferred_element_type=jnp.float32)
-            hid[:, cols] = (g / (1.0 + jnp.exp(-g)) * u).astype(jnp.bfloat16)
-
-        loads[4].wait()
-        loads[5].wait()
+
+        def products(k, cp):
+            cp.wait_recv()
+            for ld in loads[4 * k : 4 * k + 4]:
+                ld.wait()
+            span_k = slice(k * kc, (k + 1) * kc)
+
+            @pl.loop(0, ff // tn)
+            def _(n):
+                cols = pl.ds(pl.multiple_of(n * tn, tn), tn)
+                x0 = xb[0, k, :, :kc]
+                x1 = xb[1, k, :, :kc]
+                g = jnp.dot(x0, wg[0, span_k, cols], preferred_element_type=jnp.float32)
+                g = g + jnp.dot(x1, wg[1, span_k, cols], preferred_element_type=jnp.float32)
+                u = jnp.dot(x0, wu[0, span_k, cols], preferred_element_type=jnp.float32)
+                u = u + jnp.dot(x1, wu[1, span_k, cols], preferred_element_type=jnp.float32)
+                if k > 0:
+                    g = g + acc_g[:, cols]
+                    u = u + acc_u[:, cols]
+                if k < PIECES - 1:
+                    acc_g[:, cols] = g
+                    acc_u[:, cols] = u
+                else:
+                    hid[:, cols] = (g / (1.0 + jnp.exp(-g)) * u).astype(jnp.bfloat16)
+
+        direct(0)
+        for k in range(1, PIECES):
+            direct(k)
+            products(k - 1, across(k - 1))
+        products(PIECES - 1, across(PIECES - 1))
+
+        loads[-2].wait()
+        loads[-1].wait()
         span = n_grp * n_tp // experts
         expert = (grp * n_tp + tp) // span
-        table = xb[0, :, half:].astype(jnp.float32)
+        table = xb[0, PIECES - 1, :, kc:].astype(jnp.float32)
         lanes = lax.broadcasted_iota(jnp.int32, table.shape, 1)
         weight = jnp.sum(jnp.where(lanes == expert, table, 0.0), axis=1, keepdims=True)
         half_rows = n_a * rows
@@ -146,7 +166,7 @@
         def stage_x(j, cp):
             cp.wait_recv()
             sx[j] = (pown[j, theirs, :].astype(jnp.float32) + r0[j, theirs, :].astype(jnp.float32)).astype(jnp.bfloat16)
-            xp = remote(sx.at[j], r1.at[j], x_send.at[n_a + j], x_recv.at[j], x_peer)
+            xp = remote(sx.at[j], r1.at[j], y_send.at[j], x_recv.at[j], x_peer)
             xp.start()
             return xp
 
@@ -161,7 +181,7 @@
             for d in range(n_a):
                 to_a = lax.rem(a + d, n_a)
                 zp = remote(
-                    block(tbuf, j, to_a), ra.at[j, a], z_send.at[j, d], z_recv.at[j, a], line(0, to_a)
+                    tbuf.at[j, pl.ds(pl.multiple_of(to_a * rows, rows), rows), :], ra.at[j, a], z_send.at[j, d], z_recv.at[j, a], line(0, to_a)
                 )
                 zp.start()
                 out.append(zp)
@@ -187,46 +207,71 @@
         loads = [
             pltpu.make_async_copy(qlat_ref.at[0], ql, load_sem.at[0]),
             pltpu.make_async_copy(cache_ref.at[0], cl, load_sem.at[1]),
-            pltpu.make_async_copy(crope_ref.at[0], cr, load_sem.at[2]),
-            pltpu.make_async_copy(kvp_ref.at[0], kvw, load_sem.at[3]),
+            pltpu.make_async_copy(crope_ref.at[0], cr.at[:, :rope, :], load_sem.at[2]),
+            pltpu.make_async_copy(crope_ref.at[0], cr.at[:, rope:, :], load_sem.at[3]),
+            pltpu.make_async_copy(kvp_ref.at[0], kvw, load_sem.at[4]),
         ]
         for ld in loads:
             ld.start()
         greet()
         x = res_ref[...].astype(jnp.float32)
         scale = lax.rsqrt(jnp.mean(x * x, axis=1, keepdims=True) + NORM_EPS)
+        pos = b * n_a + a
+        sends = []
+
+        def dispatch(k):
+            for d in range(n_a):
+                to_a = lax.rem(a + d, n_a)
+                piece = msg.at[k] if k == PIECES - 1 else msg.at[k, :, :kc]
+                cp = remote(piece, block(xb, 0, k, pos), d_send.at[k, d], d_recv.at[k, pos], line(1, to_a))
+                cp.start()
+                sends.append(cp)
+
+        for k in range(PIECES):
+            cols = pl.ds(pl.multiple_of(tp * half + k * kc, 128), kc)
+            part = res_ref[:, cols].astype(jnp.float32) * scale * gain_ref[:, cols].astype(jnp.float32)
+            msg[k, :, :kc] = part.astype(jnp.bfloat16)
+        pl.semaphore_wait(barrier, n_a + 1)
+        for k in range(PIECES - 1):
+            dispatch(k)
         normed = x * scale * gain_ref[...].astype(jnp.float32)
         logits = lax.dot_general(
-            normed, router_ref[...].astype(jnp.float32), NT,
+            router_ref[...].astype(jnp.float32), normed, NT,
             precision=lax.Precision.HIGHEST, preferred_element_type=jnp.float32,
         )
         s = 1.0 / (1.0 + jnp.exp(-logits))
-        ids = lax.broadcasted_iota(jnp.int32, s.shape, 1)
+        ids = lax.broadcasted_iota(jnp.int32, s.shape, 0)
         chosen = jnp.zeros(s.shape, jnp.float32)
-        for k in range(routes_ref.shape[1]):
-            chosen = jnp.where(routes_ref[:, k : k + 1] == ids, 1.0, chosen)
+        for k in range(routes_ref.shape[0]):
+            chosen = jnp.where(routes_ref[k : k + 1, :] == ids, 1.0, chosen)
         picked = s * chosen
-        dense = ROUTE_SCALE * picked / jnp.sum(picked, axis=1, keepdims=True)
-        narrow = normed.astype(jnp.bfloat16)
-        msg[:, :half] = jnp.where(tp == 0, narrow[:, :half], narrow[:, half:])
-        msg[:, half:] = jnp.zeros((rows, 128), jnp.bfloat16)
-        msg[:, half : half + experts] = dense.astype(jnp.bfloat16)
-        pl.semaphore_wait(barrier, n_a + 1)
-        pos = b * n_a + a
-        sends = []
-        for d in range(n_a):
-            to_a = lax.rem(a + d, n_a)
-            cp = remote(msg, block(xb, 0, pos), d_send.at[d], d_recv.at[0, pos], line(1, to_a))
-            cp.start()
-            sends.append(cp)
+        dense = (ROUTE_SCALE * picked / jnp.sum(picked, axis=0, keepdims=True)).astype(jnp.bfloat16)
+        eye_r = lax.broadcasted_iota(jnp.int32, (rows, rows), 0)
+        eye_c = lax.broadcasted_iota(jnp.int32, (rows, rows), 1)
+        eye = jnp.where(eye_r == eye_c, 1.0, 0.0).astype(jnp.bfloat16)
+        dense = lax.dot_general(eye, dense, NT, preferred_element_type=jnp.float32)
+        msg[PIECES - 1, :, kc:] = jnp.zeros((rows, 128), jnp.bfloat16)
+        msg[PIECES - 1, :, kc : kc + experts] = dense.astype(jnp.bfloat16)
+        dispatch(PIECES - 1)
 
         for ld in loads:
             ld.wait()
+
+        heads = ql.shape[1]
+        head_id = lax.broadcasted_iota(jnp.int32, (heads, 2 * rope), 0)
+        lane_id = lax.broadcasted_iota(jnp.int32, (heads, 2 * rope), 1)
+        for t in range(rows):
+            fold = jnp.zeros((heads, 2 * rope), jnp.float32)
+            for i in range(heads // 2):
+                pair = qrope_ref[t : t + 1, i * 2 * rope : (i + 1) * 2 * rope].astype(jnp.float32)
+                owner = jnp.where(lane_id < rope, 2 * i, 2 * i + 1)
+                fold = jnp.where(head_id == owner, pair, fold)
+            qr[t] = fold.astype(jnp.bfloat16)
 
         @pl.loop(0, rows)
         def _(t):
             sc = lax.dot_general(ql[t], cl[t], NT, preferred_element_type=jnp.float32)
-            sc = sc + jnp.dot(qrope_ref[t], cr[t], preferred_element_type=jnp.float32)
+            sc = sc + jnp.dot(qr[t], cr[t], preferred_element_type=jnp.float32)
             sc = sc * SCORE_SCALE
             usable = lax.broadcasted_iota(jnp.int32, sc.shape, 1) < len_ref[t]
             sc = jnp.where(usable, sc, -1e30)
@@ -236,6 +281,17 @@
             l_acc[t] = jnp.broadcast_to(jnp.sum(wts, axis=1, keepdims=True), sc.shape)
             o_acc[t] = jnp.dot(wts.astype(jnp.bfloat16), cl[t], preferred_element_type=jnp.float32)
 
+        wide = (rows, 2 * rope)
+        lane = lax.broadcasted_iota(jnp.int32, wide, 1)
+        step = (lane % (rope // 2)).astype(jnp.float32)
+        freq = jnp.exp(-(2.0 * step / rope) * math.log(ROPE_BASE))
+        row_id = lax.broadcasted_iota(jnp.int32, wide, 0)
+        position = jnp.zeros(wide, jnp.float32)
+        for t in range(rows):
+            position = jnp.where(row_id == t, len_ref[t].astype(jnp.float32), position)
+        angle = position * freq
+        cosine = jnp.cos(angle)
+        sine = jnp.where(lane < rope // 2, -jnp.sin(angle), jnp.sin(angle))
         kv = jnp.zeros((rows, kvwid), jnp.float32)
         sq = jnp.zeros((rows, 1), jnp.float32)
         for j in range(CHUNKS):
@@ -269,25 +325,17 @@
         fresh = (latent * lscale * kvgain_ref[...].astype(jnp.float32)).astype(jnp.bfloat16)
         nlat_ref[...] = fresh
         rot = both[:, lat:] * norm
-        lane = lax.broadcasted_iota(jnp.int32, rot.shape, 1)
-        step = jnp.where(lane < rope // 2, lane, lane - rope // 2).astype(jnp.float32)
-        freq = jnp.exp(-(2.0 * step / rope) * math.log(ROPE_BASE))
-        row_id = lax.broadcasted_iota(jnp.int32, rot.shape, 0)
-        position = jnp.zeros(rot.shape, jnp.float32)
-        for t in range(rows):
-            position = jnp.where(row_id == t, len_ref[t].astype(jnp.float32), position)
-        angle = position * freq
         up_part = pltpu.roll(rot, 128 - rope // 2, 1)
         down_part = pltpu.roll(rot, rope // 2, 1)
-        turned = rot * jnp.cos(angle) + jnp.where(lane < rope // 2, -up_part, down_part) * jnp.sin(angle)
-        turned = turned[:, :rope].astype(jnp.bfloat16)
-        nrope_ref[...] = turned
+        turned = rot * cosine + jnp.where(lane < rope // 2, up_part, down_part) * sine
+        nrope_ref[...] = turned[:, :rope].astype(jnp.bfloat16)
+        turned = jnp.where(lane < rope, turned, pltpu.roll(turned, rope, 1)).astype(jnp.bfloat16)
         fresh_f = fresh.astype(jnp.float32)
         turned_f = turned.astype(jnp.float32)
         for t in range(rows):
             fl = fresh_f[t : t + 1]
             own = jnp.sum(ql[t].astype(jnp.float32) * fl, axis=1, keepdims=True)
-            own = own + jnp.sum(qrope_ref[t].astype(jnp.float32) * turned_f[t : t + 1], axis=1, keepdims=True)
+            own = own + jnp.sum(qr[t].astype(jnp.float32) * turned_f[t : t + 1], axis=1, keepdims=True)
             own = own * SCORE_SCALE
             m_old = m_acc[t, :, :1]
             peak = jnp.maximum(m_old, own)
@@ -304,6 +352,15 @@
             cp.wait_send()
 
 
+def hand_over(*refs):
+    sem = refs[-1]
+    copies = [pltpu.make_async_copy(refs[i], refs[4 + i], sem.at[i]) for i in range(4)]
+    for cp in copies:
+        cp.start()
+    for cp in copies:
+        cp.wait()
+
+
 def body(
     residual, moe_gain, router, routes, gate_w, up_w, down_w, attn_gain, kv_proj, kv_gain,
     cache_latent, cache_rope, lengths, query_latent, query_rope,
@@ -314,6 +371,7 @@
     rows, width = residual.shape[1:]
     half = width // 2
     cw = half // CHUNKS
+    kc = half // PIECES
     ff = gate_w.shape[2]
     all_rows = n_grp * rows
     lat = kv_gain.shape[1]
@@ -323,7 +381,6 @@
     bf, f32 = jnp.bfloat16, jnp.float32
     vmem, smem, hbm = (pl.BlockSpec(memory_space=s) for s in (pltpu.VMEM, pltpu.SMEM, pl.ANY))
     dma = pltpu.SemaphoreType.DMA
-    q_rot = query_rope[0].reshape(rows, heads, rope)
     outs = pl.pallas_call(
         functools.partial(kernel, n_grp, n_tp),
         out_shape=(
@@ -335,8 +392,8 @@
         in_specs=[vmem] * 6 + [smem, vmem] + [hbm] * 7,
         out_specs=(vmem,) * 4,
         scratch_shapes=[
-            pltpu.VMEM((rows, half + 128), bf),
-            pltpu.VMEM((2, all_rows, half + 128), bf),
+            pltpu.VMEM((PIECES, rows, kc + 128), bf),
+            pltpu.VMEM((2, PIECES, all_rows, kc + 128), bf),
             pltpu.VMEM((2, half, ff), bf),
             pltpu.VMEM((2, half, ff), bf),
             pltpu.VMEM((2, ff, half), bf),
@@ -356,16 +413,19 @@
             pltpu.VMEM((rows, lat + 128), f32),
             pltpu.VMEM(kv_proj.shape[1:], bf),
             pltpu.VMEM(cache_latent.shape[1:], bf),
-            pltpu.VMEM(cache_rope.shape[1:], bf),
+            pltpu.VMEM((rows, 2 * rope, slots), bf),
+            pltpu.VMEM((rows, heads, 2 * rope), bf),
             pltpu.VMEM(query_latent.shape[1:], bf),
             pltpu.VMEM((rows, heads, lat), f32),
             pltpu.VMEM((rows, heads, slots), f32),
             pltpu.VMEM((rows, heads, slots), f32),
-            dma((6,)),
-            dma((n_a,)),
-            dma((2, n_grp)),
-            dma((2, n_a)),
-            dma((n_a + CHUNKS,)),
+            dma((4 * PIECES + 2,)),
+            dma((PIECES, n_a)),
+            dma((PIECES, n_grp)),
+            dma((PIECES,)),
+            dma((PIECES,)),
+            dma((PIECES, n_a)),
+            dma((CHUNKS,)),
             dma((CHUNKS,)),
             dma((CHUNKS,)),
             dma((CHUNKS,)),
@@ -379,10 +439,18 @@
             collective_id=0, has_side_effects=True, vmem_limit_bytes=63 * 1024 * 1024
         ),
     )(
-        residual[0], moe_gain, router[0], routes[0], attn_gain, kv_gain, lengths[0], q_rot,
+        residual[0], moe_gain, router[0], routes[0].T, attn_gain, kv_gain, lengths[0], query_rope[0],
         gate_w, up_w, down_w, kv_proj, cache_latent, cache_rope, query_latent,
     )
-    return tuple(o[None] for o in outs)
+    final = pl.pallas_call(
+        hand_over,
+        out_shape=tuple(jax.ShapeDtypeStruct(o.shape, bf) for o in outs),
+        in_specs=[hbm] * 4,
+        out_specs=(hbm,) * 4,
+        scratch_shapes=[dma((4,))],
+        compiler_params=pltpu.CompilerParams(vmem_limit_bytes=63 * 1024 * 1024),
+    )(*outs)
+    return tuple(o[None] for o in final)
 
 
 def solution(mesh):

time: 66.9 us -> 80.1 us (1.20)
  Pallas kernels: 56.7 us -> 79.3 us
  local copies, waits for them, and re-layouts: 9.16 us -> 0 us
    pallas_call x0 -> x1, Pallas kernels: none -> 24.6 us  [body(): pl.pallas_call(hand_over, out_shape=tuple((jax.ShapeDtypeStruct(o.shape,...]
    unnamed x4 -> x0, local copies, waits for them, and re-layouts: 6.11 us -> none
    pallas_call x1, Pallas kernels: 56.7 us -> 54.8 us  [body(): pl.pallas_call(functools.partial(kernel, n_grp, n_tp), out_shape=(jax.Sha...]
    another operation x1 -> x0, local copies, waits for them, and re-layouts: 1.69 us -> none  [body(): q_rot = query_rope[0].reshape(rows, heads, rope)]
    squeeze x1 -> x0, local copies, waits for them, and re-layouts: 1.36 us -> none  [body(): routes[0]]
where the time goes in v2:
time: 80.1 us; the launch traced here: 80 us
  Pallas kernels  79.3 us (99%)
    pallas_call x1, Pallas kernels, body(): pl.pallas_call(functools.partial(kernel, n_grp, n_tp), out_shape=(jax.Sha...  54.8 us
    pallas_call x1, Pallas kernels, body(): pl.pallas_call(hand_over, out_shape=tuple((jax.ShapeDtypeStruct(o.shape,...  24.6 us

profile of v2, /device:TPU:1, one launch (start us, length us, event | category | flops | bytes accessed | tf_op | source)
XLA Modules:
  0.0 80.0 jit_solution(8203953589069412358)
XLA Ops:
  0.6 54.8 %shard_map.174 = (bf16[16,7168]{1,0:T(8,128)(2,1)}, bf16[16,512]{1,0:T(8,128)(2,1)}, bf16[16,64]{1,0:T(8,128)(2,1)}, bf16[16,32,512]{2,1,0:T(8,128)(2,1)}) custom-call(bf16[16,7168]{1,0:T(8,128)(2,1)} %bitcast.11, bf16[1,7168]{1,0:T(2,128)(2,1)} %gain_ref.1, bf16[16,7168]{1,0:T(8,128)(2,1)} %bitcast.12, s32[8,16]{1,0:T(8,128)} %bitcast.14, ...), custom_call_target="tpu_custom_call" | custom-call | tf_op jit(solution)/shard_map/pallas_call | solution.py:384
  55.4 24.6 %shard_map.175 = (bf16[16,7168]{1,0:T(8,128)(2,1)}, bf16[16,512]{1,0:T(8,128)(2,1)}, bf16[16,64]{1,0:T(8,128)(2,1)}, bf16[16,32,512]{2,1,0:T(8,128)(2,1)}) custom-call(bf16[16,7168]{1,0:T(8,128)(2,1)} %get-tuple-element.12.refs_0_, bf16[16,512]{1,0:T(8,128)(2,1)} %get-tuple-element.13.refs_1_, bf16[16,64]{1,0:T(8,128)(2,1)} %get-tuple-element.14.refs_2_, ...), custom_call_target="tpu_custom_call" | custom-call | tf_op jit(solution)/shard_map/pallas_call | solution.py:445

commit v3 on v2

--- a/solution.py
+++ b/solution.py
@@ -14,7 +14,7 @@
 SCORE_SCALE = 192.0 ** (-0.5)
 MESH = pl.DeviceIdType.MESH
 CHUNKS = 7
-PIECES = 4
+PIECES = 7
 NT = (((1,), (1,)), ((), ()))
 
 
@@ -65,6 +65,8 @@
 
     @pl.when(side == 1)
     def _():
+        greet()
+        pl.semaphore_signal(barrier, inc=1, device_id=x_peer, device_id_type=MESH)
         own = pl.multiple_of(tp * half, 128)
         oth = pl.multiple_of((1 - tp) * half, 128)
         loads = []
@@ -84,8 +86,6 @@
             )
         for ld in loads:
             ld.start()
-        greet()
-        pl.semaphore_signal(barrier, inc=1, device_id=x_peer, device_id_type=MESH)
         pl.semaphore_wait(barrier, n_a + 2)
 
         sends = []
@@ -109,37 +109,38 @@
             sends.append(cp)
             return cp
 
-        tn = min(256, ff)
-
-        def products(k, cp):
-            cp.wait_recv()
-            for ld in loads[4 * k : 4 * k + 4]:
-                ld.wait()
+        tn = min(512, ff)
+
+        def products(k, i):
+            loads[4 * k + 2 * i].wait()
+            loads[4 * k + 2 * i + 1].wait()
             span_k = slice(k * kc, (k + 1) * kc)
 
             @pl.loop(0, ff // tn)
             def _(n):
                 cols = pl.ds(pl.multiple_of(n * tn, tn), tn)
-                x0 = xb[0, k, :, :kc]
-                x1 = xb[1, k, :, :kc]
-                g = jnp.dot(x0, wg[0, span_k, cols], preferred_element_type=jnp.float32)
-                g = g + jnp.dot(x1, wg[1, span_k, cols], preferred_element_type=jnp.float32)
-                u = jnp.dot(x0, wu[0, span_k, cols], preferred_element_type=jnp.float32)
-                u = u + jnp.dot(x1, wu[1, span_k, cols], preferred_element_type=jnp.float32)
-                if k > 0:
+                xk = xb[i, k, :, :kc]
+                g = jnp.dot(xk, wg[i, span_k, cols], preferred_element_type=jnp.float32)
+                u = jnp.dot(xk, wu[i, span_k, cols], preferred_element_type=jnp.float32)
+                if k + i > 0:
                     g = g + acc_g[:, cols]
                     u = u + acc_u[:, cols]
-                if k < PIECES - 1:
+                if k + i < PIECES:
                     acc_g[:, cols] = g
                     acc_u[:, cols] = u
                 else:
                     hid[:, cols] = (g / (1.0 + jnp.exp(-g)) * u).astype(jnp.bfloat16)
 
         direct(0)
-        for k in range(1, PIECES):
-            direct(k)
-            products(k - 1, across(k - 1))
-        products(PIECES - 1, across(PIECES - 1))
+        for k in range(PIECES):
+            cp = across(k)
+            if 0 < k < PIECES - 1:
+                direct(k + 1)
+            products(k, 0)
+            if k == 0:
+                direct(1)
+            cp.wait_recv()
+            products(k, 1)
 
         loads[-2].wait()
         loads[-1].wait()
@@ -211,9 +212,9 @@
             pltpu.make_async_copy(crope_ref.at[0], cr.at[:, rope:, :], load_sem.at[3]),
             pltpu.make_async_copy(kvp_ref.at[0], kvw, load_sem.at[4]),
         ]
+        greet()
         for ld in loads:
             ld.start()
-        greet()
         x = res_ref[...].astype(jnp.float32)
         scale = lax.rsqrt(jnp.mean(x * x, axis=1, keepdims=True) + NORM_EPS)
         pos = b * n_a + a
@@ -331,18 +332,25 @@
         nrope_ref[...] = turned[:, :rope].astype(jnp.bfloat16)
         turned = jnp.where(lane < rope, turned, pltpu.roll(turned, rope, 1)).astype(jnp.bfloat16)
         fresh_f = fresh.astype(jnp.float32)
-        turned_f = turned.astype(jnp.float32)
+        flat = rows * heads
+        own = lax.dot_general(ql[...].reshape(flat, lat), fresh, NT, preferred_element_type=jnp.float32)
+        own = own + lax.dot_general(
+            qr[...].reshape(flat, 2 * rope), turned, NT, preferred_element_type=jnp.float32
+        )
+        own_row = lax.broadcasted_iota(jnp.int32, own.shape, 0) // heads
+        own_col = lax.broadcasted_iota(jnp.int32, own.shape, 1)
+        own = jnp.sum(jnp.where(own_row == own_col, own, 0.0), axis=1, keepdims=True) * SCORE_SCALE
+        m_old = m_acc[...].reshape(flat, m_acc.shape[2])[:, :1]
+        l_old = l_acc[...].reshape(flat, l_acc.shape[2])[:, :1]
+        peak = jnp.maximum(m_old, own)
+        keep = jnp.exp(m_old - peak)
+        ow = jnp.exp(own - peak)
+        inv = 1.0 / (l_old * keep + ow)
+        keep = keep * inv
+        ow = ow * inv
         for t in range(rows):
-            fl = fresh_f[t : t + 1]
-            own = jnp.sum(ql[t].astype(jnp.float32) * fl, axis=1, keepdims=True)
-            own = own + jnp.sum(qr[t].astype(jnp.float32) * turned_f[t : t + 1], axis=1, keepdims=True)
-            own = own * SCORE_SCALE
-            m_old = m_acc[t, :, :1]
-            peak = jnp.maximum(m_old, own)
-            keep = jnp.exp(m_old - peak)
-            ow = jnp.exp(own - peak)
-            inv = 1.0 / (l_acc[t, :, :1] * keep + ow)
-            attn_ref[t] = (o_acc[t] * (keep * inv) + (ow * inv) * fl).astype(jnp.bfloat16)
+            at = slice(t * heads, (t + 1) * heads)
+            attn_ref[t] = (o_acc[t] * keep[at] + ow[at] * fresh_f[t : t + 1]).astype(jnp.bfloat16)
         for j in range(CHUNKS):
             here = hr.at[j]
             remote(here, here, h_send.at[j], h_recv.at[j], core_peer).wait_recv()
@@ -353,11 +361,15 @@
 
 
 def hand_over(*refs):
-    sem = refs[-1]
-    copies = [pltpu.make_async_copy(refs[i], refs[4 + i], sem.at[i]) for i in range(4)]
-    for cp in copies:
+    ins, outs, held, sem = refs[:4], refs[4:8], refs[8:12], refs[12]
+    first = [pltpu.make_async_copy(ins[i], held[i], sem.at[0, i]) for i in range(4)]
+    second = [pltpu.make_async_copy(held[i], outs[i], sem.at[1, i]) for i in range(4)]
+    for cp in first:
         cp.start()
-    for cp in copies:
+    for into, out in zip(first, second):
+        into.wait()
+        out.start()
+    for cp in second:
         cp.wait()
 
 
@@ -447,7 +459,7 @@
         out_shape=tuple(jax.ShapeDtypeStruct(o.shape, bf) for o in outs),
         in_specs=[hbm] * 4,
         out_specs=(hbm,) * 4,
-        scratch_shapes=[dma((4,))],
+        scratch_shapes=[pltpu.VMEM(o.shape, bf) for o in outs] + [dma((2, 4))],
         compiler_params=pltpu.CompilerParams(vmem_limit_bytes=63 * 1024 * 1024),
     )(*outs)
     return tuple(o[None] for o in final)

time: 80.1 us -> 64.4 us (0.80)
  Pallas kernels: 79.3 us -> 63.6 us
    pallas_call x1, Pallas kernels: 24.6 us -> 2.05 us  [body(): pl.pallas_call(hand_over, out_shape=tuple((jax.ShapeDtypeStruct(o.shape,...]
    pallas_call x1, Pallas kernels: 54.8 us -> 61.6 us  [body(): pl.pallas_call(functools.partial(kernel, n_grp, n_tp), out_shape=(jax.Sha...]
where the time goes in v3:
time: 64.4 us; the launch traced here: 64.3 us
  Pallas kernels  63.6 us (99%)
  between operations  0.65 us (1%)
    pallas_call x1, Pallas kernels, body(): pl.pallas_call(functools.partial(kernel, n_grp, n_tp), out_shape=(jax.Sha...  61.6 us
    pallas_call x1, Pallas kernels, body(): pl.pallas_call(hand_over, out_shape=tuple((jax.ShapeDtypeStruct(o.shape,...  2.05 us

profile of v3, /device:TPU:1, one launch (start us, length us, event | category | flops | bytes accessed | tf_op | source)
XLA Modules:
  0.0 64.3 jit_solution(528795848104044657)
XLA Ops:
  0.6 61.6 %shard_map.174 = (bf16[16,7168]{1,0:T(8,128)(2,1)}, bf16[16,512]{1,0:T(8,128)(2,1)}, bf16[16,64]{1,0:T(8,128)(2,1)}, bf16[16,32,512]{2,1,0:T(8,128)(2,1)}) custom-call(bf16[16,7168]{1,0:T(8,128)(2,1)} %bitcast.11, bf16[1,7168]{1,0:T(2,128)(2,1)} %gain_ref.1, bf16[16,7168]{1,0:T(8,128)(2,1)} %bitcast.12, s32[8,16]{1,0:T(8,128)} %bitcast.14, ...), custom_call_target="tpu_custom_call" | custom-call | tf_op jit(solution)/shard_map/pallas_call | solution.py:396
  62.2 2.1 %shard_map.175 = (bf16[16,7168]{1,0:T(8,128)(2,1)}, bf16[16,512]{1,0:T(8,128)(2,1)}, bf16[16,64]{1,0:T(8,128)(2,1)}, bf16[16,32,512]{2,1,0:T(8,128)(2,1)}) custom-call(bf16[16,7168]{1,0:T(8,128)(2,1)} %get-tuple-element.12.refs_0_, bf16[16,512]{1,0:T(8,128)(2,1)} %get-tuple-element.13.refs_1_, bf16[16,64]{1,0:T(8,128)(2,1)} %get-tuple-element.14.refs_2_, ...), custom_call_target="tpu_custom_call" | custom-call | tf_op jit(solution)/shard_map/pallas_call | solution.py:457

commit v4 on v3

--- a/solution.py
+++ b/solution.py
@@ -14,7 +14,7 @@
 SCORE_SCALE = 192.0 ** (-0.5)
 MESH = pl.DeviceIdType.MESH
 CHUNKS = 7
-PIECES = 7
+PIECES = 4
 NT = (((1,), (1,)), ((), ()))
 
 
@@ -109,38 +109,37 @@
             sends.append(cp)
             return cp
 
-        tn = min(512, ff)
-
-        def products(k, i):
-            loads[4 * k + 2 * i].wait()
-            loads[4 * k + 2 * i + 1].wait()
+        tn = min(256, ff)
+
+        def products(k, cp):
+            cp.wait_recv()
+            for ld in loads[4 * k : 4 * k + 4]:
+                ld.wait()
             span_k = slice(k * kc, (k + 1) * kc)
 
             @pl.loop(0, ff // tn)
             def _(n):
                 cols = pl.ds(pl.multiple_of(n * tn, tn), tn)
-                xk = xb[i, k, :, :kc]
-                g = jnp.dot(xk, wg[i, span_k, cols], preferred_element_type=jnp.float32)
-                u = jnp.dot(xk, wu[i, span_k, cols], preferred_element_type=jnp.float32)
-                if k + i > 0:
+                x0 = xb[0, k, :, :kc]
+                x1 = xb[1, k, :, :kc]
+                g = jnp.dot(x0, wg[0, span_k, cols], preferred_element_type=jnp.float32)
+                g = g + jnp.dot(x1, wg[1, span_k, cols], preferred_element_type=jnp.float32)
+                u = jnp.dot(x0, wu[0, span_k, cols], preferred_element_type=jnp.float32)
+                u = u + jnp.dot(x1, wu[1, span_k, cols], preferred_element_type=jnp.float32)
+                if k > 0:
                     g = g + acc_g[:, cols]
                     u = u + acc_u[:, cols]
-                if k + i < PIECES:
+                if k < PIECES - 1:
                     acc_g[:, cols] = g
                     acc_u[:, cols] = u
                 else:
                     hid[:, cols] = (g / (1.0 + jnp.exp(-g)) * u).astype(jnp.bfloat16)
 
         direct(0)
-        for k in range(PIECES):
-            cp = across(k)
-            if 0 < k < PIECES - 1:
-                direct(k + 1)
-            products(k, 0)
-            if k == 0:
-                direct(1)
-            cp.wait_recv()
-            products(k, 1)
+        for k in range(1, PIECES):
+            direct(k)
+            products(k - 1, across(k - 1))
+        products(PIECES - 1, across(PIECES - 1))
 
         loads[-2].wait()
         loads[-1].wait()

time: 64.4 us -> 58.1 us (0.902)
  Pallas kernels: 63.6 us -> 57.2 us
    pallas_call x1, Pallas kernels: 61.6 us -> 55.2 us  [body(): pl.pallas_call(functools.partial(kernel, n_grp, n_tp), out_shape=(jax.Sha...]
where the time goes in v4:
time: 58.1 us; the launch traced here: 57.9 us
  Pallas kernels  57.2 us (98%)
  between operations  0.65 us (1%)
    pallas_call x1, Pallas kernels, body(): pl.pallas_call(functools.partial(kernel, n_grp, n_tp), out_shape=(jax.Sha...  55.2 us
    pallas_call x1, Pallas kernels, body(): pl.pallas_call(hand_over, out_shape=tuple((jax.ShapeDtypeStruct(o.shape,...  2.05 us

profile of v4, /device:TPU:1, one launch (start us, length us, event | category | flops | bytes accessed | tf_op | source)
XLA Modules:
  0.0 57.9 jit_solution(11198953460574389053)
XLA Ops:
  0.6 55.2 %shard_map.174 = (bf16[16,7168]{1,0:T(8,128)(2,1)}, bf16[16,512]{1,0:T(8,128)(2,1)}, bf16[16,64]{1,0:T(8,128)(2,1)}, bf16[16,32,512]{2,1,0:T(8,128)(2,1)}) custom-call(bf16[16,7168]{1,0:T(8,128)(2,1)} %bitcast.11, bf16[1,7168]{1,0:T(2,128)(2,1)} %gain_ref.1, bf16[16,7168]{1,0:T(8,128)(2,1)} %bitcast.12, s32[8,16]{1,0:T(8,128)} %bitcast.14, ...), custom_call_target="tpu_custom_call" | custom-call | tf_op jit(solution)/shard_map/pallas_call | solution.py:395
  55.8 2.1 %shard_map.175 = (bf16[16,7168]{1,0:T(8,128)(2,1)}, bf16[16,512]{1,0:T(8,128)(2,1)}, bf16[16,64]{1,0:T(8,128)(2,1)}, bf16[16,32,512]{2,1,0:T(8,128)(2,1)}) custom-call(bf16[16,7168]{1,0:T(8,128)(2,1)} %get-tuple-element.12.refs_0_, bf16[16,512]{1,0:T(8,128)(2,1)} %get-tuple-element.13.refs_1_, bf16[16,64]{1,0:T(8,128)(2,1)} %get-tuple-element.14.refs_2_, ...), custom_call_target="tpu_custom_call" | custom-call | tf_op jit(solution)/shard_map/pallas_call | solution.py:456
